TPU v7x, 128 devices: a whole 4x4x4 slice. The times are simulated.
128 devices in a mesh: band: 8 (over x, y_lo), row: 16 (over z, y_hi, core).
Axes of the slice: x: 4, y: 4 (y_hi: 2, y_lo: 2; y = y_hi * 2 + y_lo), z: 4, core: 2. Of those that a mesh axis runs over, the one named last changes fastest.
Arguments:
- phase: float32 [4096, 4096], P('row'), may hold values from -3.140625 to 3.140625
- aperture: int32 [4096, 4096], P('row'), may hold values 0 or 1
- defocus_index: int32 [16], P('band'), may hold values from 0 to 3
- intensity: float32 [16, 512, 512], P('band', 'row'), may hold values from 0.1 to 3
Outputs:
- gradient: float32 [4096, 4096], P('row', 'band')
All inputs are finite; a program needn't handle non-finite values. No bound on the sum of `aperture` on one device may be relied on, other than what follows from the above.
Results may differ from a plain program's by a relative error of at most 0.0032.
Values may be sent and summed in bfloat16 or wider, within the bound.
No kernel may reach another device: no remote copies, remote signals or barrier semaphores. Data moves between devices by JAX's collectives and lax.ppermute only.
A program may use at most 128 MiB of HBM per device.

v0:
```python
import math
import jax
import jax.numpy as jnp
from jax import lax
from jax.sharding import PartitionSpec as P

defocus_strength = math.pi


def focal_table(wave_index, waves, focal_width, pupil_width):
    scale_ratio = 1.0 / (1.0 + wave_index.astype(jnp.float32) / waves)
    column = 2 * lax.broadcasted_iota(jnp.int32, (focal_width, pupil_width), 1) - pupil_width + 1
    offset = 2 * lax.broadcasted_iota(jnp.int32, (focal_width, pupil_width), 0) - focal_width
    phase_angle = (column * offset).astype(jnp.float32) * (
        scale_ratio * (math.pi / (4.0 * pupil_width))
    )
    normalizer = 1.0 / math.sqrt(pupil_width)
    return jnp.stack(
        [jnp.cos(phase_angle) * normalizer, -jnp.sin(phase_angle) * normalizer]
    ).astype(jnp.bfloat16)


def pupil_field(phase, aperture, defocus_level, first_row, pupil_width):
    row_pos = (
        2 * (first_row + lax.broadcasted_iota(jnp.int32, phase.shape, 0)) - pupil_width + 1
    ).astype(jnp.float32)
    col_pos = (2 * lax.broadcasted_iota(jnp.int32, phase.shape, 1) - pupil_width + 1).astype(
        jnp.float32
    )
    radius = (row_pos * row_pos + col_pos * col_pos) / float(pupil_width * pupil_width)
    shifted = phase + defocus_level.astype(jnp.float32) * defocus_strength * radius
    amplitude = aperture.astype(jnp.float32)
    return (amplitude * jnp.cos(shifted), amplitude * jnp.sin(shifted))


def pupil_products(pupil_pair, table):
    blocks = lax.dot_general(
        pupil_pair, table, (((2,), (2,)), ((), ())), preferred_element_type=jnp.float32
    )
    real_part = blocks[0, :, 0] - blocks[1, :, 1]
    imag_part = blocks[0, :, 1] + blocks[1, :, 0]
    return jnp.stack([real_part, imag_part]).astype(jnp.bfloat16)


def focal_rows(products, table_cols):
    blocks = lax.dot_general(
        products, table_cols, (((1,), (2,)), ((), ())), preferred_element_type=jnp.float32
    )
    real_part = blocks[0, :, 0] - blocks[1, :, 1]
    imag_part = blocks[0, :, 1] + blocks[1, :, 0]
    return jnp.concatenate([real_part, imag_part], axis=1)


def back_rows(weighted, table_cols):
    unit_count = weighted.shape[0]
    table_width = table_cols.shape[1]
    halves = weighted.reshape(unit_count, 2, table_width)
    blocks = lax.dot_general(
        halves, table_cols, (((2,), (1,)), ((), ())), preferred_element_type=jnp.float32
    )
    real_part = blocks[:, 0, 0] + blocks[:, 1, 1]
    imag_part = blocks[:, 1, 0] - blocks[:, 0, 1]
    return jnp.stack([real_part, imag_part]).astype(jnp.bfloat16)


def phase_gradient(back, table, field_re, field_im):
    blocks = lax.dot_general(
        back, table, (((1,), (1,)), ((), ())), preferred_element_type=jnp.float32
    )
    spread_re = blocks[0, :, 0] + blocks[1, :, 1]
    spread_im = blocks[1, :, 0] - blocks[0, :, 1]
    return spread_im * field_re - spread_re * field_im


def local(phase, aperture, defocus_index, intensity):
    row_count = phase.shape[0]
    pupil_width = phase.shape[1]
    local_waves = intensity.shape[0]
    focal_width = intensity.shape[2]
    first_row = lax.axis_index("row") * row_count
    band_start = lax.axis_index("band") * local_waves
    total_waves = local_waves * lax.axis_size("band")
    running = jnp.zeros((row_count, pupil_width), jnp.float32)
    for member in range(local_waves):
        wave_index = band_start + member
        table = focal_table(wave_index, total_waves, focal_width, pupil_width)
        field_re, field_im = pupil_field(
            phase, aperture, defocus_index[member], first_row, pupil_width
        )
        pupil_pair = jnp.stack([field_re, field_im]).astype(jnp.bfloat16)
        products = pupil_products(pupil_pair, table)
        table_cols = lax.dynamic_slice_in_dim(table, first_row, row_count, 2)
        focal = lax.psum_scatter(
            focal_rows(products, table_cols), "row", scatter_dimension=0, tiled=True
        )
        focal_re = focal[:, :focal_width]
        focal_im = focal[:, focal_width:]
        misfit = focal_re * focal_re + focal_im * focal_im - intensity[member]
        weighted = jnp.concatenate([misfit * focal_re, misfit * focal_im], axis=1).astype(
            jnp.bfloat16
        )
        back = back_rows(lax.all_gather(weighted, "row", axis=0, tiled=True), table_cols)
        gradient = phase_gradient(back, table, field_re, field_im)
        running = running + gradient
    return lax.psum_scatter(running, "band", scatter_dimension=1, tiled=True)


def solution(mesh):
    return jax.shard_map(
        local,
        mesh=mesh,
        in_specs=(P("row", None), P("row", None), P("band"), P("band", "row", None)),
        out_specs=P("row", "band"),
        check_vma=False,
    )
```

profile of v0, /device:TPU:1, one launch (start us, length us, event | category | flops | bytes accessed | tf_op | source)
XLA Modules:
  0.0 509.1 jit_solution(2497417982271974181)
XLA Ops:
  6.5 0.0 reduce-scatter.12.cloned.1.call-start
  6.7 1.3 fusion.75
  9.3 0.0 copy-start.8
  9.3 0.0 copy-start.10
  9.3 62.6 %multiply_convert_fusion.3 = (bf16[1,512,4096]{2,1,0:T(8,128)(2,1)}, bf16[1,512,4096]{2,1,0:T(8,128)(2,1)S(1)}, bf16[1,512,4096]{2,1,0:T(8,128)(2,1)S(1)}, bf16[1,512,4096]{2,1,0:T(8,128)(2,1)}) fusion(f32[]{:T(128)S(6)} %mul.229, s32[512]{0:T(512)S(1)} %multiply_add_fusion.1, s32[4096]{0:T(1024)S(1)} %multiply_add_fusion, f32[]{:T(128)S(6)} %mul.246), kind=kLoop, calls=%fused_computation.11 | loop fusion | flops 29360128 | bytes 16795656 | tf_op jit(solution)/shard_map/convert.26
  71.9 31.9 %convert_bitcast_fusion.3 = (bf16[1,256,4096]{2,1,0:T(8,128)(2,1)}, bf16[1,256,4096]{2,1,0:T(8,128)(2,1)}, bf16[1,256,4096]{2,1,0:T(8,128)(2,1)S(1)}, bf16[1,256,4096]{2,1,0:T(8,128)(2,1)S(1)}) fusion(f32[256,4096]{1,0:T(8,128)S(1)} %copy-done.8, f32[]{:T(128)} %bitcast, f32[4096]{0:T(1024)S(1)} %convert_multiply_fusion.2, ...), kind=kLoop, calls=%fused_computation.52 | loop fusion | flops 14680064 | bytes 16794632 | tf_op jit(solution)/shard_map/stack | solution.py:90
  103.8 4.5 fusion.8
  108.3 0.2 fusion.61
  108.5 1.7 fusion.46
  110.3 0.5 fusion.28
  110.7 0.2 pad_maximum_fusion.3
  110.9 1.9 copy.59
  112.8 0.0 reduce-scatter.12.cloned.1.call-update
  112.8 0.0 reduce-scatter.10.cloned.1.call-start
  112.9 9.3 %fusion.4 = f32[2,256,2,512]{3,1,2,0:T(8,128)S(1)} fusion(bf16[1,512,4096]{2,1,0:T(8,128)(2,1)} %get-tuple-element.30, bf16[1,512,4096]{2,1,0:T(8,128)(2,1)} %get-tuple-element.27, bf16[1,256,4096]{2,1,0:T(8,128)(2,1)} %get-tuple-element.6, bf16[1,256,4096]{2,1,0:T(8,128)(2,1)} %get-tuple-element.5), kind=kOutput, calls=%fused_computation.17 | convolution fusion | flops 4320133120 | bytes 14680064 | tf_op jit(solution)/shard_map/dot_general | solution.py:37
  122.2 0.2 fusion.57
  122.4 0.7 fusion.41
  123.1 0.5 fusion.30
  123.6 0.2 pad_maximum_fusion.2
  123.8 0.0 copy-start.12
  123.8 1.8 copy.57
  125.6 0.0 reduce-scatter.10.cloned.1.call-update
  125.6 0.0 all-gather.5.cloned.1.call-start
  125.7 59.7 %reduce-scatter.12.cloned.1.call-done = f32[32,1024]{1,0:T(8,128)} async-done(((f32[512,1024]{1,0:T(8,128)}), f32[32,1024]{1,0:T(8,128)}) %reduce-scatter.12.cloned.1.call-update) | async-done | bytes 131088 | tf_op jit(solution)/shard_map/reduce_scatter | solution.py:93
  185.4 74.5 %reduce-scatter.10.cloned.1.call-done = f32[32,1024]{1,0:T(8,128)} async-done(((f32[512,1024]{1,0:T(8,128)}), f32[32,1024]{1,0:T(8,128)}) %reduce-scatter.10.cloned.1.call-update) | async-done | bytes 131088 | tf_op jit(solution)/shard_map/reduce_scatter | solution.py:93
  259.9 1.0 multiply_convert_fusion.7
  260.9 0.6 pad_maximum_fusion.5
  261.5 0.0 all-gather.5.cloned.1.call-update
  261.5 0.0 all-gather.3.cloned.1.call-start
  261.6 0.6 pad_maximum_fusion.4
  262.2 0.0 all-gather.3.cloned.1.call-update
  262.2 0.0 reduce-scatter.8.cloned.1.call-start
  262.3 46.4 %all-gather.5.cloned.1.call-done = bf16[512,1024]{1,0:T(8,128)(2,1)} async-done(((bf16[32,1024]{1,0:T(8,128)(2,1)}), bf16[512,1024]{1,0:T(8,128)(2,1)}) %all-gather.5.cloned.1.call-update) | async-done | bytes 1048592 | tf_op jit(solution)/shard_map/all_gather | solution.py:102
  308.7 1.5 copy.38
  310.2 1.8 fusion.51
  312.0 0.1 fusion.63
  312.1 42.6 %all-gather.3.cloned.1.call-done = bf16[512,1024]{1,0:T(8,128)(2,1)} async-done(((bf16[32,1024]{1,0:T(8,128)(2,1)}), bf16[512,1024]{1,0:T(8,128)(2,1)}) %all-gather.3.cloned.1.call-update) | async-done | bytes 1048592 | tf_op jit(solution)/shard_map/all_gather | solution.py:102
  354.7 1.5 copy.33
  356.2 0.0 copy-start.5
  356.2 1.9 fusion.54
  358.1 0.1 fusion.59
  358.2 0.3 copy-done.5
  358.5 1.3 copy-done.7
  359.8 8.2 %fusion.2 = f32[2,256,2,4096]{3,1,2,0:T(8,128)} fusion(bf16[1,512,4096]{2,1,0:T(8,128)(2,1)S(1)} %copy-done.7, bf16[1,512,4096]{2,1,0:T(8,128)(2,1)S(1)} %copy-done.5, bf16[1,512,256]{2,1,0:T(8,128)(2,1)S(1)} %get-tuple-element.14, bf16[1,512,256]{2,1,0:T(8,128)(2,1)S(1)} %get-tuple-element.13), kind=kOutput, calls=%fused_computation.16 | convolution fusion | flops 4312793088 | bytes 25690112 | tf_op jit(solution)/shard_map/dot_general | solution.py:67
  368.0 8.2 %fusion.6 = f32[2,256,2,4096]{3,1,2,0:T(8,128)} fusion(bf16[1,512,4096]{2,1,0:T(8,128)(2,1)S(1)} %copy-done.3, bf16[1,512,4096]{2,1,0:T(8,128)(2,1)S(1)} %copy-done.1, bf16[1,512,256]{2,1,0:T(8,128)(2,1)S(1)} %get-tuple-element.18, bf16[1,512,256]{2,1,0:T(8,128)(2,1)S(1)} %get-tuple-element.17), kind=kOutput, calls=%fused_computation.18 | convolution fusion | flops 4312793088 | bytes 25690112 | tf_op jit(solution)/shard_map/dot_general | solution.py:67
  376.1 37.7 %fusion.15 = f32[256,4096]{1,0:T(8,128)} fusion(f32[2,256,2,4096]{3,1,2,0:T(8,128)} %fusion.6, f32[2,256,2,4096]{3,1,2,0:T(8,128)} %fusion.2, f32[256,4096]{1,0:T(8,128)S(1)} %copy-done.9, f32[]{:T(128)} %bitcast, f32[4096]{0:T(1024)S(1)} %convert_multiply_fusion.2, f32[256]{0:T(256)S(1)} %convert_multiply_fusion.3, s32[256,4096]{1,0:T(8,128)S(1)} %copy-done.11, ...), kind=kLoop, calls=%fused_computation.26 | loop fusion | flops 22020096 | bytes 46154760 | tf_op jit(solution)/shard_map/add | solution.py:104
  413.9 0.0 reduce-scatter.8.cloned.1.call-update
  413.9 88.6 %reduce-scatter.8.cloned.1.call-done = f32[256,512]{1,0:T(8,128)} async-done(((f32[256,4096]{1,0:T(8,128)}), f32[256,512]{1,0:T(8,128)}) %reduce-scatter.8.cloned.1.call-update) | async-done | bytes 524304 | tf_op jit(solution)/shard_map/reduce_scatter | solution.py:105
  (24 shorter events, 0.1 us)
Async XLA Ops:
  6.5 178.9 %reduce-scatter.12.cloned.1.call-start = ((), (), s32[]{:S(2)}) async-start(), calls=%async_computation.7 | async-start | bytes 2228224 | tf_op jit(solution)/shard_map/reduce_scatter | solution.py:93
  9.3 62.6 %copy-start.8 = (f32[256,4096]{1,0:T(8,128)S(1)}, f32[256,4096]{1,0:T(8,128)}, u32[]{:S(2)}) copy-start(f32[256,4096]{1,0:T(8,128)} %param.4) | copy-start | bytes 12582916
  9.3 62.6 %copy-start.10 = (s32[256,4096]{1,0:T(8,128)S(1)}, s32[256,4096]{1,0:T(8,128)}, u32[]{:S(2)}) copy-start(s32[256,4096]{1,0:T(8,128)} %param.5) | copy-start | bytes 12582916
  71.9 31.9 %copy-start = (bf16[1,512,4096]{2,1,0:T(8,128)(2,1)}, bf16[1,512,4096]{2,1,0:T(8,128)(2,1)S(1)}, u32[]{:S(2)}) copy-start(bf16[1,512,4096]{2,1,0:T(8,128)(2,1)S(1)} %get-tuple-element.28) | copy-start | bytes 12582916
  71.9 31.9 %copy-start.2 = (bf16[1,512,4096]{2,1,0:T(8,128)(2,1)}, bf16[1,512,4096]{2,1,0:T(8,128)(2,1)S(1)}, u32[]{:S(2)}) copy-start(bf16[1,512,4096]{2,1,0:T(8,128)(2,1)S(1)} %get-tuple-element.29) | copy-start | bytes 12582916
  112.8 147.1 %reduce-scatter.10.cloned.1.call-start = ((), (), s32[]{:S(2)}) async-start(), calls=%async_computation.6 | async-start | bytes 2228224 | tf_op jit(solution)/shard_map/reduce_scatter | solution.py:93
  112.9 9.5 %copy-start.4 = (bf16[1,512,4096]{2,1,0:T(8,128)(2,1)S(1)}, bf16[1,512,4096]{2,1,0:T(8,128)(2,1)}, u32[]{:S(2)}) copy-start(bf16[1,512,4096]{2,1,0:T(8,128)(2,1)} %get-tuple-element.27) | copy-start | bytes 12582916
  112.9 9.5 %copy-start.6 = (bf16[1,512,4096]{2,1,0:T(8,128)(2,1)S(1)}, bf16[1,512,4096]{2,1,0:T(8,128)(2,1)}, u32[]{:S(2)}) copy-start(bf16[1,512,4096]{2,1,0:T(8,128)(2,1)} %get-tuple-element.30) | copy-start | bytes 12582916
  123.8 136.1 %copy-start.12 = (f32[2,32,512]{2,1,0:T(8,128)S(1)}, f32[2,32,512]{2,1,0:T(8,128)}, u32[]{:S(2)}) copy-start(f32[2,32,512]{2,1,0:T(8,128)} %param.7) | copy-start | bytes 393220
  125.6 183.0 %all-gather.5.cloned.1.call-start = ((), (), s32[]{:S(2)}) async-start(), calls=%async_computation.4 | async-start | bytes 1114112 | tf_op jit(solution)/shard_map/all_gather | solution.py:102
  261.5 93.1 %all-gather.3.cloned.1.call-start = ((), (), s32[]{:S(2)}) async-start(), calls=%async_computation.3 | async-start | bytes 1114112 | tf_op jit(solution)/shard_map/all_gather | solution.py:102
  262.2 240.3 %reduce-scatter.8.cloned.1.call-start = ((), (), s32[]{:S(2)}) async-start(), calls=%async_computation.5 | async-start | bytes 4718592 | tf_op jit(solution)/shard_map/reduce_scatter | solution.py:105
  356.2 2.4 copy-start.5
  356.2 3.6 copy-start.7
  359.8 8.2 %copy-start.1 = (bf16[1,512,4096]{2,1,0:T(8,128)(2,1)S(1)}, bf16[1,512,4096]{2,1,0:T(8,128)(2,1)}, u32[]{:S(2)}) copy-start(bf16[1,512,4096]{2,1,0:T(8,128)(2,1)} %copy-done) | copy-start | bytes 12582916
  359.8 8.2 %copy-start.3 = (bf16[1,512,4096]{2,1,0:T(8,128)(2,1)S(1)}, bf16[1,512,4096]{2,1,0:T(8,128)(2,1)}, u32[]{:S(2)}) copy-start(bf16[1,512,4096]{2,1,0:T(8,128)(2,1)} %copy-done.2) | copy-start | bytes 12582916
  368.0 8.2 %copy-start.9 = (f32[256,4096]{1,0:T(8,128)S(1)}, f32[256,4096]{1,0:T(8,128)}, u32[]{:S(2)}) copy-start(f32[256,4096]{1,0:T(8,128)} %param.4) | copy-start | bytes 12582916
  368.0 8.2 %copy-start.11 = (s32[256,4096]{1,0:T(8,128)S(1)}, s32[256,4096]{1,0:T(8,128)}, u32[]{:S(2)}) copy-start(s32[256,4096]{1,0:T(8,128)} %param.5) | copy-start | bytes 12582916
Sparse Core Ops, SparseCore 0:
  112.9 72.4 reduce-scatter.11
  189.8 70.0 reduce-scatter.9
  262.4 46.2 all-gather.4
  311.0 43.6 all-gather.2
  414.0 88.4 reduce-scatter.7
where the time goes:
time: 509 us
  waiting for transfers between devices  312 us (61%)
  other arithmetic  136 us (27%)
  matrix products  36.3 us (7%)
  between operations  14.7 us (3%)
  local copies, waits for them, and re-layouts  9.65 us (2%)
    reduce_scatter x2, waiting for transfers between devices, local(): lax.psum_scatter(focal_rows(products, table_cols), 'row', scatter_dimensi...  134 us
    all_gather x2, waiting for transfers between devices, local(): lax.all_gather(weighted, 'row', axis=0, tiled=True)  89 us
    reduce_scatter x1, waiting for transfers between devices, local(): return lax.psum_scatter(running, 'band', scatter_dimension=1, tiled=True)  88.6 us
    another operation x2, other arithmetic  63.5 us
    add x1, other arithmetic, local(): running = running + gradient  37.7 us
    another operation x1, other arithmetic, local(): pupil_pair = jnp.stack([field_re, field_im]).astype(jnp.bfloat16)  31.9 us
    dot_general x2, matrix products, phase_gradient(): lax.dot_general(back, table, (((1,), (1,)), ((), ())), preferred_element_...  16.3 us
    dot_general x2, matrix products, pupil_products(): lax.dot_general(pupil_pair, table, (((2,), (2,)), ((), ())), preferred_el...  13.8 us
  transfers between devices with their start and end apart: 5, of which 5 were waited for; matrix products, arithmetic and copies ran while one was open for 3% of the time, Pallas kernels for 0%

commit v1 on v0

--- a/solution.py
+++ b/solution.py
@@ -99,7 +99,12 @@
         weighted = jnp.concatenate([misfit * focal_re, misfit * focal_im], axis=1).astype(
             jnp.bfloat16
         )
-        back = back_rows(lax.all_gather(weighted, "row", axis=0, tiled=True), table_cols)
+        back = back_rows(
+            jnp.concatenate(
+                lax.all_to_all(jnp.stack([weighted] * lax.axis_size("row")), "row", 0, 0), axis=0
+            ),
+            table_cols,
+        )
         gradient = phase_gradient(back, table, field_re, field_im)
         running = running + gradient
     return lax.psum_scatter(running, "band", scatter_dimension=1, tiled=True)

time: 509 us -> 462 us (0.908)
  waiting for transfers between devices: 312 us -> 253 us
  starting transfers between devices: 0.17 us -> 11.6 us
    all_gather x2 -> x0, waiting for transfers between devices: 89 us -> none  [local(): lax.all_gather(weighted, 'row', axis=0, tiled=True)]
    all_to_all x0 -> x2, waiting for transfers between devices: none -> 31.8 us  [local(): lax.all_to_all(jnp.stack([weighted] * lax.axis_size('row')), 'row', 0, 0)]
    all_to_all x0 -> x2, starting transfers between devices: none -> 11.5 us  [local(): lax.all_to_all(jnp.stack([weighted] * lax.axis_size('row')), 'row', 0, 0)]
where the time goes in v1:
time: 462 us
  waiting for transfers between devices  253 us (55%)
  other arithmetic  135 us (29%)
  matrix products  36.3 us (8%)
  between operations  14.8 us (3%)
  starting transfers between devices  11.6 us (3%)
  local copies, waits for them, and re-layouts  10.7 us (2%)
    reduce_scatter x2, waiting for transfers between devices, local(): lax.psum_scatter(focal_rows(products, table_cols), 'row', scatter_dimensi...  134 us
    reduce_scatter x1, waiting for transfers between devices, local(): return lax.psum_scatter(running, 'band', scatter_dimension=1, tiled=True)  87.4 us
    another operation x2, other arithmetic  63.5 us
    add x1, other arithmetic, local(): running = running + gradient  37.7 us
    another operation x1, other arithmetic, local(): pupil_pair = jnp.stack([field_re, field_im]).astype(jnp.bfloat16)  31.9 us
    all_to_all x2, waiting for transfers between devices, local(): lax.all_to_all(jnp.stack([weighted] * lax.axis_size('row')), 'row', 0, 0)  31.8 us
    dot_general x2, matrix products, phase_gradient(): lax.dot_general(back, table, (((1,), (1,)), ((), ())), preferred_element_...  16.3 us
    dot_general x2, matrix products, pupil_products(): lax.dot_general(pupil_pair, table, (((2,), (2,)), ((), ())), preferred_el...  13.8 us
  transfers between devices with their start and end apart: 5, of which 5 were waited for; matrix products, arithmetic and copies ran while one was open for 3% of the time, Pallas kernels for 0%

profile of v1, /device:TPU:1, one launch (start us, length us, event | category | flops | bytes accessed | tf_op | source)
XLA Modules:
  0.0 461.8 jit_solution(15885560212896807333)
XLA Ops:
  6.5 0.0 reduce-scatter.12.cloned.1.call-start
  6.7 1.4 fusion.77
  9.4 0.0 copy-start.8
  9.4 0.0 copy-start.10
  9.4 62.6 %multiply_convert_fusion.3 = (bf16[1,512,4096]{2,1,0:T(8,128)(2,1)}, bf16[1,512,4096]{2,1,0:T(8,128)(2,1)S(1)}, bf16[1,512,4096]{2,1,0:T(8,128)(2,1)S(1)}, bf16[1,512,4096]{2,1,0:T(8,128)(2,1)}) fusion(f32[]{:T(128)S(6)} %mul.229, s32[512]{0:T(512)S(1)} %multiply_add_fusion.1, s32[4096]{0:T(1024)S(1)} %multiply_add_fusion, f32[]{:T(128)S(6)} %mul.246), kind=kLoop, calls=%fused_computation.11 | loop fusion | flops 29360128 | bytes 16795656 | tf_op jit(solution)/shard_map/convert.26
  72.0 0.0 copy-done.8
  72.0 0.0 copy-done.10
  72.0 31.9 %convert_bitcast_fusion.3 = (bf16[1,256,4096]{2,1,0:T(8,128)(2,1)}, bf16[1,256,4096]{2,1,0:T(8,128)(2,1)}, bf16[1,256,4096]{2,1,0:T(8,128)(2,1)S(1)}, bf16[1,256,4096]{2,1,0:T(8,128)(2,1)S(1)}) fusion(f32[256,4096]{1,0:T(8,128)S(1)} %copy-done.8, f32[]{:T(128)} %bitcast, f32[4096]{0:T(1024)S(1)} %convert_multiply_fusion.2, ...), kind=kLoop, calls=%fused_computation.52 | loop fusion | flops 14680064 | bytes 16794632 | tf_op jit(solution)/shard_map/stack | solution.py:90
  103.9 0.0 copy-done.4
  103.9 4.5 fusion.8
  108.4 0.2 fusion.63
  108.6 1.7 fusion.50
  110.3 0.5 fusion.28
  110.8 0.2 pad_maximum_fusion.3
  111.0 1.9 copy.55
  112.9 0.0 reduce-scatter.12.cloned.1.call-update
  112.9 0.0 reduce-scatter.10.cloned.1.call-start
  113.0 9.3 %fusion.4 = f32[2,256,2,512]{3,1,2,0:T(8,128)S(1)} fusion(bf16[1,512,4096]{2,1,0:T(8,128)(2,1)} %get-tuple-element.30, bf16[1,512,4096]{2,1,0:T(8,128)(2,1)} %get-tuple-element.27, bf16[1,256,4096]{2,1,0:T(8,128)(2,1)} %get-tuple-element.6, bf16[1,256,4096]{2,1,0:T(8,128)(2,1)} %get-tuple-element.5), kind=kOutput, calls=%fused_computation.17 | convolution fusion | flops 4320133120 | bytes 14680064 | tf_op jit(solution)/shard_map/dot_general | solution.py:37
  122.3 0.2 fusion.59
  122.5 0.7 fusion.45
  123.2 0.5 fusion.30
  123.7 0.2 pad_maximum_fusion.2
  123.9 0.0 copy-start.12
  123.9 1.8 copy.53
  125.7 0.0 reduce-scatter.10.cloned.1.call-update
  125.7 59.8 %reduce-scatter.12.cloned.1.call-done = f32[32,1024]{1,0:T(8,128)} async-done(((f32[512,1024]{1,0:T(8,128)}), f32[32,1024]{1,0:T(8,128)}) %reduce-scatter.12.cloned.1.call-update) | async-done | bytes 131088 | tf_op jit(solution)/shard_map/reduce_scatter | solution.py:93
  185.5 74.5 %reduce-scatter.10.cloned.1.call-done = f32[32,1024]{1,0:T(8,128)} async-done(((f32[512,1024]{1,0:T(8,128)}), f32[32,1024]{1,0:T(8,128)}) %reduce-scatter.10.cloned.1.call-update) | async-done | bytes 131088 | tf_op jit(solution)/shard_map/reduce_scatter | solution.py:93
  260.0 1.0 multiply_convert_fusion.7
  261.0 1.2 stack.45
  262.2 7.1 %all-to-all-start = ((bf16[16,32,1024]{2,1,0:T(8,128)(2,1)}), bf16[16,32,1024]{2,1,0:T(8,128)(2,1)S(1)}, u32[]{:S(2)}, u32[]{:S(2)}) async-start(bf16[16,32,1024]{2,1,0:T(8,128)(2,1)} %stack.45), calls=%async_computation | async-start | bytes 2097152 | tf_op jit(solution)/shard_map/all_to_all | solution.py:104
  269.3 17.2 %all-to-all-done = bf16[16,32,1024]{2,1,0:T(8,128)(2,1)S(1)} async-done(((bf16[16,32,1024]{2,1,0:T(8,128)(2,1)}), bf16[16,32,1024]{2,1,0:T(8,128)(2,1)S(1)}, u32[]{:S(2)}, u32[]{:S(2)}) %all-to-all-start) | async-done | bytes 1048608 | tf_op jit(solution)/shard_map/all_to_all | solution.py:104
  286.5 1.2 stack.52
  287.7 4.4 all-to-all-start.1
  292.1 0.0 reduce-scatter.8.cloned.1.call-start
  292.1 0.8 reshape_reshape.6
  292.9 1.7 fusion.33
  294.7 0.1 fusion.61
  294.8 14.6 %all-to-all-done.1 = bf16[16,32,1024]{2,1,0:T(8,128)(2,1)S(1)} async-done(((bf16[16,32,1024]{2,1,0:T(8,128)(2,1)}), bf16[16,32,1024]{2,1,0:T(8,128)(2,1)S(1)}, u32[]{:S(2)}, u32[]{:S(2)}) %all-to-all-start.1) | async-done | bytes 1048608 | tf_op jit(solution)/shard_map/all_to_all | solution.py:104
  309.4 0.8 reshape_reshape.7
  310.2 1.9 fusion.31
  312.1 0.1 fusion.65
  312.2 0.3 copy-done.5
  312.5 1.3 copy-done.7
  313.8 8.1 %fusion.6 = f32[2,256,2,4096]{3,1,2,0:T(8,128)} fusion(bf16[1,512,4096]{2,1,0:T(8,128)(2,1)S(1)} %copy-done.7, bf16[1,512,4096]{2,1,0:T(8,128)(2,1)S(1)} %copy-done.5, bf16[1,512,256]{2,1,0:T(8,128)(2,1)S(1)} %get-tuple-element.18, bf16[1,512,256]{2,1,0:T(8,128)(2,1)S(1)} %get-tuple-element.17), kind=kOutput, calls=%fused_computation.18 | convolution fusion | flops 4312793088 | bytes 25690112 | tf_op jit(solution)/shard_map/dot_general | solution.py:67
  322.0 8.2 %fusion.2 = f32[2,256,2,4096]{3,1,2,0:T(8,128)} fusion(bf16[1,512,4096]{2,1,0:T(8,128)(2,1)S(1)} %copy-done.3, bf16[1,512,4096]{2,1,0:T(8,128)(2,1)S(1)} %copy-done.1, bf16[1,512,256]{2,1,0:T(8,128)(2,1)S(1)} %get-tuple-element.14, bf16[1,512,256]{2,1,0:T(8,128)(2,1)S(1)} %get-tuple-element.13), kind=kOutput, calls=%fused_computation.16 | convolution fusion | flops 4312793088 | bytes 25690112 | tf_op jit(solution)/shard_map/dot_general | solution.py:67
  330.2 37.7 %fusion.15 = f32[256,4096]{1,0:T(8,128)} fusion(f32[2,256,2,4096]{3,1,2,0:T(8,128)} %fusion.6, f32[2,256,2,4096]{3,1,2,0:T(8,128)} %fusion.2, f32[256,4096]{1,0:T(8,128)S(1)} %copy-done.9, f32[]{:T(128)} %bitcast, f32[4096]{0:T(1024)S(1)} %convert_multiply_fusion.2, f32[256]{0:T(256)S(1)} %convert_multiply_fusion.3, s32[256,4096]{1,0:T(8,128)S(1)} %copy-done.11, ...), kind=kLoop, calls=%fused_computation.26 | loop fusion | flops 22020096 | bytes 46154760 | tf_op jit(solution)/shard_map/add | solution.py:109
  367.9 0.0 reduce-scatter.8.cloned.1.call-update
  367.9 87.4 %reduce-scatter.8.cloned.1.call-done = f32[256,512]{1,0:T(8,128)} async-done(((f32[256,4096]{1,0:T(8,128)}), f32[256,512]{1,0:T(8,128)}) %reduce-scatter.8.cloned.1.call-update) | async-done | bytes 524304 | tf_op jit(solution)/shard_map/reduce_scatter | solution.py:110
  (24 shorter events, 0.1 us)
Async XLA Ops:
  6.5 179.0 %reduce-scatter.12.cloned.1.call-start = ((), (), s32[]{:S(2)}) async-start(), calls=%async_computation.7 | async-start | bytes 2228224 | tf_op jit(solution)/shard_map/reduce_scatter | solution.py:93
  9.4 62.6 %copy-start.8 = (f32[256,4096]{1,0:T(8,128)S(1)}, f32[256,4096]{1,0:T(8,128)}, u32[]{:S(2)}) copy-start(f32[256,4096]{1,0:T(8,128)} %param.4) | copy-start | bytes 12582916
  9.4 62.6 %copy-start.10 = (s32[256,4096]{1,0:T(8,128)S(1)}, s32[256,4096]{1,0:T(8,128)}, u32[]{:S(2)}) copy-start(s32[256,4096]{1,0:T(8,128)} %param.5) | copy-start | bytes 12582916
  72.0 31.9 %copy-start.4 = (bf16[1,512,4096]{2,1,0:T(8,128)(2,1)}, bf16[1,512,4096]{2,1,0:T(8,128)(2,1)S(1)}, u32[]{:S(2)}) copy-start(bf16[1,512,4096]{2,1,0:T(8,128)(2,1)S(1)} %get-tuple-element.28) | copy-start | bytes 12582916
  72.0 31.9 %copy-start.6 = (bf16[1,512,4096]{2,1,0:T(8,128)(2,1)}, bf16[1,512,4096]{2,1,0:T(8,128)(2,1)S(1)}, u32[]{:S(2)}) copy-start(bf16[1,512,4096]{2,1,0:T(8,128)(2,1)S(1)} %get-tuple-element.29) | copy-start | bytes 12582916
  112.9 147.1 %reduce-scatter.10.cloned.1.call-start = ((), (), s32[]{:S(2)}) async-start(), calls=%async_computation.6 | async-start | bytes 2228224 | tf_op jit(solution)/shard_map/reduce_scatter | solution.py:93
  113.0 9.5 %copy-start = (bf16[1,512,4096]{2,1,0:T(8,128)(2,1)S(1)}, bf16[1,512,4096]{2,1,0:T(8,128)(2,1)}, u32[]{:S(2)}) copy-start(bf16[1,512,4096]{2,1,0:T(8,128)(2,1)} %get-tuple-element.27) | copy-start | bytes 12582916
  113.0 9.5 %copy-start.2 = (bf16[1,512,4096]{2,1,0:T(8,128)(2,1)S(1)}, bf16[1,512,4096]{2,1,0:T(8,128)(2,1)}, u32[]{:S(2)}) copy-start(bf16[1,512,4096]{2,1,0:T(8,128)(2,1)} %get-tuple-element.30) | copy-start | bytes 12582916
  123.9 136.1 %copy-start.12 = (f32[2,32,512]{2,1,0:T(8,128)S(1)}, f32[2,32,512]{2,1,0:T(8,128)}, u32[]{:S(2)}) copy-start(f32[2,32,512]{2,1,0:T(8,128)} %param.7) | copy-start | bytes 393220
  262.2 24.4 %all-to-all-start = ((bf16[16,32,1024]{2,1,0:T(8,128)(2,1)}), bf16[16,32,1024]{2,1,0:T(8,128)(2,1)S(1)}, u32[]{:S(2)}, u32[]{:S(2)}) async-start(bf16[16,32,1024]{2,1,0:T(8,128)(2,1)} %stack.45), calls=%async_computation | async-start | bytes 2097152 | tf_op jit(solution)/shard_map/all_to_all | solution.py:104
  287.7 21.6 %all-to-all-start.1 = ((bf16[16,32,1024]{2,1,0:T(8,128)(2,1)}), bf16[16,32,1024]{2,1,0:T(8,128)(2,1)S(1)}, u32[]{:S(2)}, u32[]{:S(2)}) async-start(bf16[16,32,1024]{2,1,0:T(8,128)(2,1)} %stack.52), calls=%async_computation.1 | async-start | bytes 2097152 | tf_op jit(solution)/shard_map/all_to_all | solution.py:104
  292.1 163.2 %reduce-scatter.8.cloned.1.call-start = ((), (), s32[]{:S(2)}) async-start(), calls=%async_computation.5 | async-start | bytes 4718592 | tf_op jit(solution)/shard_map/reduce_scatter | solution.py:110
  310.2 2.4 copy-start.5
  310.2 3.6 copy-start.7
  313.8 8.1 %copy-start.1 = (bf16[1,512,4096]{2,1,0:T(8,128)(2,1)S(1)}, bf16[1,512,4096]{2,1,0:T(8,128)(2,1)}, u32[]{:S(2)}) copy-start(bf16[1,512,4096]{2,1,0:T(8,128)(2,1)} %get-tuple-element.27) | copy-start | bytes 12582916
  313.8 8.1 %copy-start.3 = (bf16[1,512,4096]{2,1,0:T(8,128)(2,1)S(1)}, bf16[1,512,4096]{2,1,0:T(8,128)(2,1)}, u32[]{:S(2)}) copy-start(bf16[1,512,4096]{2,1,0:T(8,128)(2,1)} %get-tuple-element.30) | copy-start | bytes 12582916
  322.0 8.2 %copy-start.9 = (f32[256,4096]{1,0:T(8,128)S(1)}, f32[256,4096]{1,0:T(8,128)}, u32[]{:S(2)}) copy-start(f32[256,4096]{1,0:T(8,128)} %param.4) | copy-start | bytes 12582916
  322.0 8.2 %copy-start.11 = (s32[256,4096]{1,0:T(8,128)S(1)}, s32[256,4096]{1,0:T(8,128)}, u32[]{:S(2)}) copy-start(s32[256,4096]{1,0:T(8,128)} %param.5) | copy-start | bytes 12582916
Sparse Core Ops, SparseCore 0:
  113.0 72.4 reduce-scatter.11
  189.9 70.0 reduce-scatter.9
  368.0 87.1 reduce-scatter.7
